TPU v7x, 256 devices: a whole 4x4x8 slice. The times are simulated.
256 devices in a mesh: seq: 64 (over y, z, core), tp: 4 (over x).
Axes of the slice: x: 4, y: 4, z: 8, core: 2. Of those that a mesh axis runs over, the one named last changes fastest.
Arguments:
- signal: float32 [32, 1048576], P(None, ('seq', 'tp')), may hold values from -6 to 6
- filter_taps: float32 [32, 1048576], P(None, ('seq', 'tp')), as said below
- skip_gain: float32 [32], P('tp'), may hold values from -4 to 4
Outputs:
- output: float32 [32, 1048576], P('tp', 'seq')
Inputs may be any that keep to these rules, and one draw needn't show every extreme that they name: `filter_taps`: filter taps are real values of both signs.
All inputs are finite; a program needn't handle non-finite values.
Results may differ from a plain program's by a relative error of at most 0.000082.
Values sent between devices are 32-bit elements; how exact they have to be, the bound alone decides.
No kernel may reach another device: no remote copies, remote signals or barrier semaphores. Data moves between devices by JAX's collectives and lax.ppermute only.
A program may use at most 64 MiB of HBM per device.

v0:
```python
import math
import jax
import jax.numpy as jnp
from jax import lax
from jax.sharding import PartitionSpec as P

HIGHEST = lax.Precision.HIGHEST
block_radix = 128


def phase_table(product, modulus):
    angle = (product % modulus).astype(jnp.float32) * (2.0 * math.pi / modulus)
    return (jnp.cos(angle), jnp.sin(angle))


def rotate_sum(pattern, spectrum, tables, turn_sign):
    real_part, imag_part = spectrum
    cosine, sine_table = tables
    cos_real = jnp.einsum(pattern, real_part, cosine, precision=HIGHEST)
    cos_imag = jnp.einsum(pattern, imag_part, cosine, precision=HIGHEST)
    sin_real = jnp.einsum(pattern, real_part, sine_table, precision=HIGHEST)
    sin_imag = jnp.einsum(pattern, imag_part, sine_table, precision=HIGHEST)
    return (cos_real - turn_sign * sin_imag, cos_imag + turn_sign * sin_real)


def rotate(spectrum, tables, turn_sign):
    real_part, imag_part = spectrum
    cosine, sine_table = tables
    return (
        real_part * cosine - turn_sign * imag_part * sine_table,
        imag_part * cosine + turn_sign * real_part * sine_table,
    )


def body(signal, filter_taps, skip_gain):
    seq_count = lax.axis_size("seq")
    seq_index = lax.axis_index("seq")
    tp_count = lax.axis_size("tp")
    channels = signal.shape[0] // tp_count
    slab_signal, slab_filter = (
        lax.all_to_all(signal, "tp", split_axis=0, concat_axis=1, tiled=True),
        lax.all_to_all(filter_taps, "tp", split_axis=0, concat_axis=1, tiled=True),
    )
    slab_rows = jnp.concatenate([slab_signal, slab_filter], axis=0)
    all_rows = slab_rows.shape[0]
    tokens = slab_rows.shape[1]
    block_width = tokens // seq_count
    freq_rows = 2 * seq_count
    fft_length = freq_rows * tokens
    inner_count = tokens // block_radix
    row_index = jnp.arange(freq_rows, dtype=jnp.int32)
    token_index = jnp.arange(block_width, dtype=jnp.int32) + seq_index * block_width
    shift_table = phase_table(row_index[:, None] * token_index[None, :], fft_length)
    source_rows = (
        jnp.arange(2, dtype=jnp.int32)[:, None] * seq_count
        + jnp.arange(seq_count, dtype=jnp.int32)[None, :]
    )
    zero_block = jnp.zeros_like(slab_rows)
    padded = jnp.stack([jnp.stack([slab_rows, zero_block]), jnp.stack([zero_block, zero_block])])
    pieces = lax.all_to_all(
        padded.reshape(2, 2, all_rows, 1, seq_count, block_width),
        "seq",
        split_axis=4,
        concat_axis=3,
        tiled=True,
    )
    columns = pieces.reshape(2, 2, all_rows, seq_count, block_width)
    tables = phase_table(source_rows[:, :, None] * row_index[None, None, :], freq_rows)
    spectrum = rotate_sum("hxjm,hjk->xkm", (columns[0], columns[1]), tables, -1.0)
    spectrum = rotate(spectrum, shift_table, -1.0)
    stacked = jnp.stack(spectrum).reshape(2, all_rows, freq_rows, 1, block_width)
    row_planes = lax.all_to_all(stacked, "seq", split_axis=2, concat_axis=3, tiled=True)
    planes = row_planes.reshape(2, all_rows, 2, inner_count, block_radix)
    inner_range = jnp.arange(inner_count, dtype=jnp.int32)
    radix_range = jnp.arange(block_radix, dtype=jnp.int32)
    outer_table = phase_table(inner_range[:, None] * inner_range[None, :], inner_count)
    radix_table = phase_table(radix_range[:, None] * radix_range[None, :], block_radix)
    twist_table = phase_table(inner_range[:, None] * radix_range[None, :], tokens)
    spectrum = rotate_sum("xrba,bk->xrka", (planes[0], planes[1]), outer_table, -1.0)
    spectrum = rotate(spectrum, twist_table, -1.0)
    spectrum = rotate_sum("xrka,ac->xrkc", spectrum, radix_table, -1.0)
    sig_real, sig_imag = (spectrum[0][:channels], spectrum[1][:channels])
    fil_real, fil_imag = (spectrum[0][channels:], spectrum[1][channels:])
    spectrum = (
        sig_real * fil_real - sig_imag * fil_imag,
        sig_real * fil_imag + sig_imag * fil_real,
    )
    spectrum = rotate_sum("xrkc,ca->xrka", spectrum, radix_table, 1.0)
    spectrum = rotate(spectrum, twist_table, 1.0)
    spectrum = rotate_sum("xrka,kb->xrba", spectrum, outer_table, 1.0)
    inverse = jnp.stack(spectrum).reshape(2, channels, 2, seq_count, block_width)
    gathered = lax.all_to_all(inverse, "seq", split_axis=3, concat_axis=2, tiled=True)
    gathered = gathered.reshape(2, channels, freq_rows, block_width)
    spectrum = rotate((gathered[0], gathered[1]), shift_table, 1.0)
    tables = phase_table(row_index[:, None, None] * source_rows[None, :, :], freq_rows)
    spectrum = rotate_sum("xkm,khj->xhjm", spectrum, tables, 1.0)
    stacked = jnp.stack(spectrum).reshape(2, channels, 2, seq_count, 1, block_width)
    arrived = lax.all_to_all(stacked, "seq", split_axis=3, concat_axis=4, tiled=True)
    result = arrived[0, :, 0].reshape(channels, tokens)
    return result / fft_length + skip_gain[:, None] * slab_signal


def solution(mesh):
    placed = (P(None, ("seq", "tp")), P(None, ("seq", "tp")), P("tp"))
    return jax.shard_map(
        body, mesh=mesh, in_specs=placed, out_specs=P("tp", "seq"), check_vma=False
    )
```

profile of v0, /device:TPU:1, one launch (start us, length us, event | category | flops | bytes accessed | tf_op | source)
XLA Modules:
  0.0 445.9 jit_solution(14319236365581633981)
XLA Ops:
  0.0 12.5 %all_to_all.89 = f32[4,8,4096]{2,1,0:T(8,128)S(1)} all-to-all(f32[4,8,4096]{2,1,0:T(8,128)} %bitcast.228), channel_id=1, replica_groups=mesh['seq'=64,'tp'=4] {'tp'}, dimensions={0} | all-to-all | bytes 1048576 | tf_op jit(solution)/shard_map/all_to_all | solution.py:41
  12.5 10.4 %all_to_all.90 = f32[4,8,4096]{2,1,0:T(8,128)S(1)} all-to-all(f32[4,8,4096]{2,1,0:T(8,128)} %bitcast.229), channel_id=1, replica_groups=mesh['seq'=64,'tp'=4] {'tp'}, dimensions={0} | all-to-all | bytes 1048576 | tf_op jit(solution)/shard_map/all_to_all | solution.py:42
  24.6 5.2 %copy.40 = f32[2,2,16,1,64,256]{5,1,2,3,0,4:T(2,128)} copy(f32[2,2,16,1,64,256]{5,4,2,1,0,3:T(8,128)S(1)} %bitcast.221) | data formatting | bytes 8388608 | tf_op jit(solution)/shard_map/reshape | solution.py:61
  29.8 16.7 %all-to-all-start.2 = ((f32[2,2,16,1,64,256]{5,1,2,3,0,4:T(2,128)}), f32[2,2,16,1,64,256]{5,1,2,3,0,4:T(2,128)}, u32[]{:S(2)}, u32[]{:S(2)}) async-start(f32[2,2,16,1,64,256]{5,1,2,3,0,4:T(2,128)} %copy.40), calls=%async_computation.2 | async-start | bytes 8388608 | tf_op jit(solution)/shard_map/all_to_all | solution.py:60
  47.2 94.8 %all-to-all-done.2 = f32[2,2,16,1,64,256]{5,1,2,3,0,4:T(2,128)} async-done(((f32[2,2,16,1,64,256]{5,1,2,3,0,4:T(2,128)}), f32[2,2,16,1,64,256]{5,1,2,3,0,4:T(2,128)}, u32[]{:S(2)}, u32[]{:S(2)}) %all-to-all-start.2) | async-done | bytes 4194336 | tf_op jit(solution)/shard_map/all_to_all | solution.py:60
  142.0 3.9 fusion.224
  145.8 3.3 fusion.10
  149.2 3.3 fusion.11
  152.5 3.5 fusion.8
  155.9 4.1 subtract_bitcast_fusion
  160.5 4.4 copy.43
  164.9 5.9 %all-to-all-start.3 = ((f32[2,16,128,1,256]{4,1,0,3,2:T(8,128)}), f32[2,16,128,1,256]{4,1,0,3,2:T(8,128)}, u32[]{:S(2)}, u32[]{:S(2)}) async-start(f32[2,16,128,1,256]{4,1,0,3,2:T(8,128)} %copy.43), calls=%async_computation.3 | async-start | bytes 8388608 | tf_op jit(solution)/shard_map/all_to_all | solution.py:72
  172.0 94.8 %all-to-all-done.3 = f32[2,16,128,1,256]{4,1,0,3,2:T(8,128)} async-done(((f32[2,16,128,1,256]{4,1,0,3,2:T(8,128)}), f32[2,16,128,1,256]{4,1,0,3,2:T(8,128)}, u32[]{:S(2)}, u32[]{:S(2)}) %all-to-all-start.3) | async-done | bytes 4194336 | tf_op jit(solution)/shard_map/all_to_all | solution.py:72
  266.8 4.6 %copy.122 = f32[2,16,64,2,1,256]{5,2,3,1,4,0:T(8,128)S(1)} copy(f32[2,16,64,2,1,256]{5,1,0,3,2,4:T(8,128)} %bitcast.30) | data formatting | bytes 8388608 | tf_op jit(solution)/shard_map/all_to_all | solution.py:72
  275.3 3.5 fusion.76
  278.7 3.0 squeeze.20
  281.8 3.8 fusion.78
  285.7 2.3 multiply_add_fusion.2
  294.7 2.4 multiply_subtract_fusion
  308.3 2.5 fusion.21
  310.8 2.5 stack.47
  313.3 3.1 copy.57
  322.6 56.8 %all_to_all.91 = f32[2,8,2,64,256]{4,2,1,0,3:T(2,128)S(1)} all-to-all(f32[2,8,2,64,256]{4,2,1,0,3:T(2,128)S(1)} %pad_maximum_fusion), channel_id=1, replica_groups=mesh['seq'=64,'tp'=4] {'seq'}, dimensions={3} | all-to-all | bytes 4194304 | tf_op jit(solution)/shard_map/all_to_all | solution.py:92
  387.8 56.9 %all_to_all.92 = f32[2,8,2,64,1,256]{5,1,2,0,4,3:T(8,128)S(1)} all-to-all(f32[2,8,2,64,1,256]{5,1,2,0,4,3:T(8,128)S(1)} %copy.64), channel_id=1, replica_groups=mesh['seq'=64,'tp'=4] {'seq'}, dimensions={3} | all-to-all | bytes 4194304 | tf_op jit(solution)/shard_map/all_to_all | solution.py:98
  (53 shorter events, 41.0 us)
Async XLA Ops:
  29.8 112.1 %all-to-all-start.2 = ((f32[2,2,16,1,64,256]{5,1,2,3,0,4:T(2,128)}), f32[2,2,16,1,64,256]{5,1,2,3,0,4:T(2,128)}, u32[]{:S(2)}, u32[]{:S(2)}) async-start(f32[2,2,16,1,64,256]{5,1,2,3,0,4:T(2,128)} %copy.40), calls=%async_computation.2 | async-start | bytes 8388608 | tf_op jit(solution)/shard_map/all_to_all | solution.py:60
  164.9 101.8 %all-to-all-start.3 = ((f32[2,16,128,1,256]{4,1,0,3,2:T(8,128)}), f32[2,16,128,1,256]{4,1,0,3,2:T(8,128)}, u32[]{:S(2)}, u32[]{:S(2)}) async-start(f32[2,16,128,1,256]{4,1,0,3,2:T(8,128)} %copy.43), calls=%async_computation.3 | async-start | bytes 8388608 | tf_op jit(solution)/shard_map/all_to_all | solution.py:72
  281.8 3.9 copy-start
  281.8 3.9 copy-start.1
  313.3 3.1 copy-start.2
  318.8 2.5 copy-start.3
  387.8 56.9 %copy-start.4 = (f32[8]{0:T(128)S(1)}, f32[8]{0:T(128)}, u32[]{:S(2)}) copy-start(f32[8]{0:T(128)} %param.5) | copy-start | bytes 100
where the time goes:
time: 451 us; the launch traced here: 446 us
  waiting for transfers between devices  190 us (42%)
  blocking collectives  137 us (30%)
  matrix products  54.8 us (12%)
  local copies, waits for them, and re-layouts  36.6 us (8%)
  starting transfers between devices  22.6 us (5%)
  other arithmetic  5.11 us (1%)
    all_to_all x1, waiting for transfers between devices, body(): lax.all_to_all(stacked, 'seq', split_axis=2, concat_axis=3, tiled=True)  94.8 us
    all_to_all x1, waiting for transfers between devices, body(): lax.all_to_all(padded.reshape(2, 2, all_rows, 1, seq_count, block_width),...  94.8 us
    all_to_all x1, blocking collectives, body(): lax.all_to_all(stacked, 'seq', split_axis=3, concat_axis=4, tiled=True)  56.9 us
    all_to_all x1, blocking collectives, body(): lax.all_to_all(inverse, 'seq', split_axis=3, concat_axis=2, tiled=True)  56.8 us
    all_to_all x1, starting transfers between devices, body(): lax.all_to_all(padded.reshape(2, 2, all_rows, 1, seq_count, block_width),...  16.7 us
    dot_general x6, matrix products, rotate_sum(): cos_imag = jnp.einsum(pattern, imag_part, cosine, precision=HIGHEST)  14.2 us
    dot_general x6, matrix products, rotate_sum(): sin_imag = jnp.einsum(pattern, imag_part, sine_table, precision=HIGHEST)  14 us
    dot_general x6, matrix products, rotate_sum(): cos_real = jnp.einsum(pattern, real_part, cosine, precision=HIGHEST)  13.7 us
  transfers between devices with their start and end apart: 2, of which 2 were waited for; matrix products, arithmetic and copies ran while one was open for 0% of the time, Pallas kernels for 0%

commit v1 on v0

--- a/solution.py
+++ b/solution.py
@@ -37,8 +37,25 @@
     seq_index = lax.axis_index("seq")
     tp_count = lax.axis_size("tp")
     channels = signal.shape[0] // tp_count
+
+    def measure_scenes(x_in):
+        lane_axis = "tp"
+        b_next, d_next = (lax.axis_size(lane_axis), lax.axis_index(lane_axis))
+        spare = list(x_in.shape)
+        inter = x_in.shape[0] // b_next
+        spare[0] = inter
+        tile_out = spare[1]
+        spare[1] = tile_out * b_next
+        high = jnp.zeros(spare, x_in.dtype)
+        for w in range(b_next):
+            tmp = lax.dynamic_slice_in_dim(x_in, (d_next ^ w) * inter, inter, axis=0)
+            if w:
+                tmp = lax.ppermute(tmp, lane_axis, tuple(((m, m ^ w) for m in range(b_next))))
+            high = lax.dynamic_update_slice_in_dim(high, tmp, (d_next ^ w) * tile_out, axis=1)
+        return high
+
     slab_signal, slab_filter = (
-        lax.all_to_all(signal, "tp", split_axis=0, concat_axis=1, tiled=True),
+        measure_scenes(signal),
         lax.all_to_all(filter_taps, "tp", split_axis=0, concat_axis=1, tiled=True),
     )
     slab_rows = jnp.concatenate([slab_signal, slab_filter], axis=0)

time: 451 us -> 446 us (0.989)
  blocking collectives: 137 us -> 114 us
  waiting for transfers between devices: 190 us -> 198 us
  starting transfers between devices: 22.6 us -> 29.7 us
    all_to_all x2 -> x0, blocking collectives: 22.9 us -> none  [the longest x1 12.5 us: body(): lax.all_to_all(signal, 'tp', split_axis=0, concat_axis=1, tiled=True)]
    ppermute x0 -> x3, starting transfers between devices: none -> 4.62 us  [measure_scenes(): lax.ppermute(tmp, lane_axis, tuple(((m, m ^ w) for m in range(b_next))))]
  transfers between devices with their start and end apart: 2 -> 6, of which waited for: 2 -> 5; matrix products, arithmetic and copies ran while one was open for 0% -> 0% of each run, Pallas kernels for 0% -> 0%
where the time goes in v1:
time: 446 us; the launch traced here: 439 us
  waiting for transfers between devices  198 us (44%)
  blocking collectives  114 us (26%)
  matrix products  54.8 us (12%)
  local copies, waits for them, and re-layouts  37.8 us (8%)
  starting transfers between devices  29.7 us (7%)
  other arithmetic  5.11 us (1%)
    all_to_all x1, waiting for transfers between devices, body(): lax.all_to_all(stacked, 'seq', split_axis=2, concat_axis=3, tiled=True)  94.8 us
    all_to_all x1, waiting for transfers between devices, body(): lax.all_to_all(padded.reshape(2, 2, all_rows, 1, seq_count, block_width),...  94.8 us
    all_to_all x1, blocking collectives, body(): lax.all_to_all(stacked, 'seq', split_axis=3, concat_axis=4, tiled=True)  56.9 us
    all_to_all x1, blocking collectives, body(): lax.all_to_all(inverse, 'seq', split_axis=3, concat_axis=2, tiled=True)  56.8 us
    all_to_all x1, starting transfers between devices, body(): lax.all_to_all(padded.reshape(2, 2, all_rows, 1, seq_count, block_width),...  15.2 us
    dot_general x6, matrix products, rotate_sum(): cos_imag = jnp.einsum(pattern, imag_part, cosine, precision=HIGHEST)  14.2 us
    dot_general x6, matrix products, rotate_sum(): sin_imag = jnp.einsum(pattern, imag_part, sine_table, precision=HIGHEST)  14 us
    dot_general x6, matrix products, rotate_sum(): cos_real = jnp.einsum(pattern, real_part, cosine, precision=HIGHEST)  13.7 us
  transfers between devices with their start and end apart: 6, of which 5 were waited for; matrix products, arithmetic and copies ran while one was open for 0% of the time, Pallas kernels for 0%

profile of v1, /device:TPU:1, one launch (start us, length us, event | category | flops | bytes accessed | tf_op | source)
XLA Modules:
  0.0 439.5 jit_solution(17964783713766148942)
XLA Ops:
  3.3 2.5 collective-permute-start.1
  5.8 3.9 all-to-all-start
  11.5 2.5 collective-permute-done.2
  14.0 3.9 all-to-all-done
  19.6 5.2 %copy.40 = f32[2,2,16,1,64,256]{5,1,2,3,0,4:T(2,128)} copy(f32[2,2,16,1,64,256]{5,4,2,1,0,3:T(8,128)S(1)} %bitcast.217) | data formatting | bytes 8388608 | tf_op jit(solution)/shard_map/reshape | solution.py:78
  24.9 15.2 %all-to-all-start.1 = ((f32[2,2,16,1,64,256]{5,1,2,3,0,4:T(2,128)}), f32[2,2,16,1,64,256]{5,1,2,3,0,4:T(2,128)}, u32[]{:S(2)}, u32[]{:S(2)}) async-start(f32[2,2,16,1,64,256]{5,1,2,3,0,4:T(2,128)} %copy.40), calls=%async_computation.1 | async-start | bytes 8388608 | tf_op jit(solution)/shard_map/all_to_all | solution.py:77
  40.7 94.8 %all-to-all-done.1 = f32[2,2,16,1,64,256]{5,1,2,3,0,4:T(2,128)} async-done(((f32[2,2,16,1,64,256]{5,1,2,3,0,4:T(2,128)}), f32[2,2,16,1,64,256]{5,1,2,3,0,4:T(2,128)}, u32[]{:S(2)}, u32[]{:S(2)}) %all-to-all-start.1) | async-done | bytes 4194336 | tf_op jit(solution)/shard_map/all_to_all | solution.py:77
  135.5 3.9 fusion.224
  139.4 3.3 fusion.10
  142.7 3.3 fusion.11
  146.0 3.5 fusion.8
  149.5 4.1 subtract_bitcast_fusion
  154.1 4.4 %copy.43 = f32[2,16,128,1,256]{4,1,0,3,2:T(8,128)} copy(f32[2,16,128,1,256]{4,2,1,0,3:T(8,128)S(1)} %maximum_bitcast_fusion) | data formatting | bytes 8388608 | tf_op jit(solution)/shard_map/reshape | solution.py:88
  158.5 5.9 %all-to-all-start.2 = ((f32[2,16,128,1,256]{4,1,0,3,2:T(8,128)}), f32[2,16,128,1,256]{4,1,0,3,2:T(8,128)}, u32[]{:S(2)}, u32[]{:S(2)}) async-start(f32[2,16,128,1,256]{4,1,0,3,2:T(8,128)} %copy.43), calls=%async_computation.2 | async-start | bytes 8388608 | tf_op jit(solution)/shard_map/all_to_all | solution.py:89
  165.6 94.8 %all-to-all-done.2 = f32[2,16,128,1,256]{4,1,0,3,2:T(8,128)} async-done(((f32[2,16,128,1,256]{4,1,0,3,2:T(8,128)}), f32[2,16,128,1,256]{4,1,0,3,2:T(8,128)}, u32[]{:S(2)}, u32[]{:S(2)}) %all-to-all-start.2) | async-done | bytes 4194336 | tf_op jit(solution)/shard_map/all_to_all | solution.py:89
  260.4 4.6 %copy.122 = f32[2,16,64,2,1,256]{5,2,3,1,4,0:T(8,128)S(1)} copy(f32[2,16,64,2,1,256]{5,1,0,3,2,4:T(8,128)} %bitcast.27) | data formatting | bytes 8388608 | tf_op jit(solution)/shard_map/all_to_all | solution.py:89
  268.9 3.4 fusion.76
  272.3 3.0 squeeze.20
  275.4 3.8 fusion.78
  301.9 2.5 fusion.21
  304.4 2.5 stack.47
  306.9 3.1 copy.57
  316.2 56.8 %all_to_all.70 = f32[2,8,2,64,256]{4,2,1,0,3:T(2,128)S(1)} all-to-all(f32[2,8,2,64,256]{4,2,1,0,3:T(2,128)S(1)} %pad_maximum_fusion), channel_id=1, replica_groups=mesh['seq'=64,'tp'=4] {'seq'}, dimensions={3} | all-to-all | bytes 4194304 | tf_op jit(solution)/shard_map/all_to_all | solution.py:109
  381.4 56.9 %all_to_all.71 = f32[2,8,2,64,1,256]{5,1,2,0,4,3:T(8,128)S(1)} all-to-all(f32[2,8,2,64,1,256]{5,1,2,0,4,3:T(8,128)S(1)} %copy.64), channel_id=1, replica_groups=mesh['seq'=64,'tp'=4] {'seq'}, dimensions={3} | all-to-all | bytes 4194304 | tf_op jit(solution)/shard_map/all_to_all | solution.py:115
  (64 shorter events, 50.9 us)
Async XLA Ops:
  1.2 8.5 %collective-permute-start = (f32[8,4096]{1,0:T(8,128)S(1)}, f32[8,4096]{1,0:T(8,128)S(1)}, u32[]{:S(2)}, u32[]{:S(2)}) collective-permute-start(f32[8,4096]{1,0:T(8,128)S(1)} %get-tuple-element.18), channel_id=1, source_target_pairs={{0,1},{1,0},{2,3},{3,2},{4,5},{5,4},{6,7},{7,6},{8,9},{9,8},{10,11... | collective-permute-start | bytes 393224 | tf_op jit(solution)/shard_map/ppermute | solution.py:53
  3.3 8.2 %collective-permute-start.1 = (f32[8,4096]{1,0:T(8,128)S(1)}, f32[8,4096]{1,0:T(8,128)S(1)}, u32[]{:S(2)}, u32[]{:S(2)}) collective-permute-start(f32[8,4096]{1,0:T(8,128)S(1)} %get-tuple-element.20), channel_id=1, source_target_pairs={{0,2},{1,3},{2,0},{3,1},{4,6},{5,7},{6,4},{7,5},{8,10},{9,11},{10,... | collective-permute-start | bytes 393224 | tf_op jit(solution)/shard_map/ppermute | solution.py:53
  5.8 8.2 %collective-permute-start.2 = (f32[8,4096]{1,0:T(8,128)S(1)}, f32[8,4096]{1,0:T(8,128)S(1)}, u32[]{:S(2)}, u32[]{:S(2)}) collective-permute-start(f32[8,4096]{1,0:T(8,128)S(1)} %get-tuple-element.17), channel_id=1, source_target_pairs={{0,3},{1,2},{2,1},{3,0},{4,7},{5,6},{6,5},{7,4},{8,11},{9,10},{10,... | collective-permute-start | bytes 393224 | tf_op jit(solution)/shard_map/ppermute | solution.py:53
  5.8 12.1 %all-to-all-start = ((f32[4,8,4096]{2,1,0:T(8,128)}), f32[4,8,4096]{2,1,0:T(8,128)S(1)}, u32[]{:S(2)}, u32[]{:S(2)}) async-start(f32[4,8,4096]{2,1,0:T(8,128)} %bitcast.222), calls=%async_computation | async-start | bytes 1048576 | tf_op jit(solution)/shard_map/all_to_all | solution.py:59
  24.9 110.7 %all-to-all-start.1 = ((f32[2,2,16,1,64,256]{5,1,2,3,0,4:T(2,128)}), f32[2,2,16,1,64,256]{5,1,2,3,0,4:T(2,128)}, u32[]{:S(2)}, u32[]{:S(2)}) async-start(f32[2,2,16,1,64,256]{5,1,2,3,0,4:T(2,128)} %copy.40), calls=%async_computation.1 | async-start | bytes 8388608 | tf_op jit(solution)/shard_map/all_to_all | solution.py:77
  158.5 101.8 %all-to-all-start.2 = ((f32[2,16,128,1,256]{4,1,0,3,2:T(8,128)}), f32[2,16,128,1,256]{4,1,0,3,2:T(8,128)}, u32[]{:S(2)}, u32[]{:S(2)}) async-start(f32[2,16,128,1,256]{4,1,0,3,2:T(8,128)} %copy.43), calls=%async_computation.2 | async-start | bytes 8388608 | tf_op jit(solution)/shard_map/all_to_all | solution.py:89
  275.3 3.9 copy-start
  275.4 3.9 copy-start.1
  306.9 3.1 copy-start.2
  312.3 2.5 copy-start.3
  381.4 56.9 %copy-start.4 = (f32[8]{0:T(128)S(1)}, f32[8]{0:T(128)}, u32[]{:S(2)}) copy-start(f32[8]{0:T(128)} %param.5) | copy-start | bytes 100
